TPU v7x, 512 devices: a whole 4x8x8 slice. The times are simulated.
512 devices in a mesh: pipe: 4 (over x), tm: 32 (over y_lo, z), dp: 4 (over y_hi, core).
Axes of the slice: x: 4, y: 8 (y_hi: 2, y_lo: 4; y = y_hi * 4 + y_lo), z: 8, core: 2. Of those that a mesh axis runs over, the one named last changes fastest.
Arguments:
- video: bfloat16 [4, 4, 64, 64, 320], P(None, 'dp', 'tm'), may hold values from -6 to 6
- cotangent: bfloat16 [4, 4, 64, 64, 320], P(None, 'dp', 'tm'), may hold values from -6 to 6
- timesteps: int32 [4, 4], P(None, 'dp'), may hold values from 0 to 999
- conv_weight: bfloat16 [4, 3, 320, 320], P('pipe'), may hold values from -0.1875 to 0.1875
- out_weight: bfloat16 [4, 320, 320], P('pipe'), may hold values from -0.3125 to 0.3125
Outputs:
- conv_grad: float32 [4, 3, 320, 320], P('pipe')
- out_grad: float32 [4, 320, 320], P('pipe')
All inputs are finite; a program needn't handle non-finite values.
Results may differ from a plain program's by a relative error of at most 0.012.
Values may be sent and summed in bfloat16 or wider, within the bound.
A program may use at most 64 MiB of HBM per device.

v0:
```python
import math
import jax
import jax.numpy as jnp
from jax import lax
from jax.sharding import PartitionSpec as P

EPSILON = 1e-06


def padded_2(block, sides, width):
    for axis, dim in sides:
        count = lax.axis_size(axis)
        forward = [(i, i + 1) for i in range(count - 1)]
        backward = [(target, source) for source, target in forward]
        low = lax.ppermute(
            lax.slice_in_dim(block, block.shape[dim] - width, None, axis=dim), axis, forward
        )
        high = lax.ppermute(lax.slice_in_dim(block, 0, width, axis=dim), axis, backward)
        block = jnp.concatenate([low, block, high], axis=dim)
    return block


def from_partner(value, axis, stride):
    mask = 2**stride
    pairs = [(source, source ^ mask) for source in range(lax.axis_size(axis))]
    return lax.ppermute(value, axis, pairs)


def from_behind(array, axis, by):
    peers = lax.axis_size(axis)
    pairs = [(i, i + by) for i in range(peers) if 0 <= i + by < peers]
    return lax.ppermute(array, axis, pairs)


def embed(times, channels):
    half = channels // 2
    index = jnp.arange(half).astype(jnp.float32)
    freq = jnp.exp(index * (-math.log(10000.0) / half))
    angle = times.astype(jnp.float32)[..., None] * freq
    return jnp.concatenate([jnp.sin(angle), jnp.cos(angle)], -1)


def prepare(inputs, emb_pair, conv_pair):
    x_float = inputs.astype(jnp.float32)
    inv_rms = lax.rsqrt(jnp.mean(x_float * x_float, -1, keepdims=True) + EPSILON)
    normed = x_float * inv_rms
    norm_low = normed.astype(jnp.bfloat16)
    padded = padded_2(norm_low, (("tm", 1),), 1)
    frames = inputs.shape[1]
    pre_act = emb_pair[:, None, None, :]
    for offset in range(3):
        pre_act = pre_act + jnp.einsum(
            "dfpc,dcx->dfpx",
            padded[:, offset : offset + frames],
            conv_pair[:, offset],
            preferred_element_type=jnp.float32,
        )
    active = jax.nn.silu(pre_act).astype(jnp.bfloat16)
    return (inv_rms, normed, padded, pre_act, active)


def body(video, cotangent, timesteps, conv_weight, out_weight):
    current_section_index = lax.axis_index("pipe")
    sections = lax.axis_size("pipe")
    final_section = sections - 1
    micro = video.shape[0]
    half_microbatch_count = micro // 2
    ticks = half_microbatch_count + sections - 1
    channels = video.shape[-1]
    frames = video.shape[2]
    bit_count = sections.bit_length() - 1
    packed = jnp.concatenate([conv_weight[0], out_weight[0][None]], 0)
    mirrored = packed
    for bit_pos in range(bit_count):
        mirrored = from_partner(mirrored, "pipe", bit_pos)
    conv_pair = jnp.stack([conv_weight[0], mirrored[:3]])
    out_pair = jnp.stack([out_weight[0], mirrored[3]])
    embedded = embed(timesteps[:, 0], channels)

    def pick(stacked, down_tick, up_tick):
        down_part = lax.dynamic_index_in_dim(
            stacked, jnp.clip(down_tick, 0, ticks - 1), 0, keepdims=False
        )[0]
        up_part = lax.dynamic_index_in_dim(
            stacked, jnp.clip(up_tick, 0, ticks - 1), 0, keepdims=False
        )[1]
        return jnp.stack([down_part, up_part])

    empty_activation = jnp.zeros(video.shape[2:], jnp.bfloat16)
    down_buf = empty_activation
    up_buf = empty_activation
    saved = []
    for current_clock_tick in range(ticks):
        down_in = down_buf
        up_in = up_buf
        if current_clock_tick < half_microbatch_count:
            down_in = jnp.where(current_section_index == 0, video[current_clock_tick, 0], down_buf)
            up_in = jnp.where(
                current_section_index == final_section,
                video[half_microbatch_count + current_clock_tick, 0],
                up_buf,
            )
        inputs = jnp.stack([down_in, up_in])
        down_row = lax.dynamic_index_in_dim(
            embedded,
            jnp.clip(current_clock_tick - current_section_index, 0, half_microbatch_count - 1),
            0,
            keepdims=False,
        )
        up_row = lax.dynamic_index_in_dim(
            embedded,
            half_microbatch_count
            + jnp.clip(
                current_clock_tick - (final_section - current_section_index),
                0,
                half_microbatch_count - 1,
            ),
            0,
            keepdims=False,
        )
        emb_pair = jnp.stack([down_row, up_row])
        inv_rms, normed, padded, pre_act, active = prepare(inputs, emb_pair, conv_pair)
        outputs = (
            inputs.astype(jnp.float32)
            + jnp.einsum("dfpc,dcx->dfpx", active, out_pair, preferred_element_type=jnp.float32)
        ).astype(jnp.bfloat16)
        saved.append((inv_rms, normed, padded, pre_act, active))
        if current_clock_tick + 1 < ticks:
            down_buf = from_behind(outputs[0], "pipe", 1)
            up_buf = from_behind(outputs[1], "pipe", -1)
    stored = jax.tree.map(lambda *leaves: jnp.stack(leaves), *saved)
    conv_acc = jnp.zeros((2, 3, channels, channels), jnp.float32)
    out_acc = jnp.zeros((2, channels, channels), jnp.float32)
    downward_gradient_holder = empty_activation
    upward_gradient_holder = empty_activation
    for current_clock_tick in range(ticks):
        down_micro = current_clock_tick - (final_section - current_section_index)
        up_micro = current_clock_tick - current_section_index
        down_valid = (down_micro >= 0) & (down_micro < half_microbatch_count)
        up_valid = (up_micro >= 0) & (up_micro < half_microbatch_count)
        downward_hidden_gradient = downward_gradient_holder
        upward_hidden_gradient = upward_gradient_holder
        if current_clock_tick < half_microbatch_count:
            downward_hidden_gradient = jnp.where(
                current_section_index == final_section,
                cotangent[current_clock_tick, 0],
                downward_gradient_holder,
            )
            upward_hidden_gradient = jnp.where(
                current_section_index == 0,
                cotangent[half_microbatch_count + current_clock_tick, 0],
                upward_gradient_holder,
            )
        downward_hidden_gradient = jnp.where(down_valid, downward_hidden_gradient, empty_activation)
        upward_hidden_gradient = jnp.where(up_valid, upward_hidden_gradient, empty_activation)
        grad_out = jnp.stack([downward_hidden_gradient, upward_hidden_gradient])
        down_tick = down_micro + current_section_index
        up_tick = up_micro + final_section - current_section_index
        inv_rms, normed, padded, pre_act, active = tuple(
            (pick(item, down_tick, up_tick) for item in stored)
        )
        out_acc = out_acc + jnp.einsum(
            "dfpc,dfpx->dcx", active, grad_out, preferred_element_type=jnp.float32
        )
        grad_act = jnp.einsum(
            "dfpx,dcx->dfpc", grad_out, out_pair, preferred_element_type=jnp.float32
        )
        sigma = jax.nn.sigmoid(pre_act)
        grad_pre = (grad_act * sigma * (1.0 + pre_act * (1.0 - sigma))).astype(jnp.bfloat16)
        grad_pad = padded_2(grad_pre, (("tm", 1),), 1)
        conv_terms = []
        grad_norm = jnp.zeros(normed.shape, jnp.float32)
        for offset in range(3):
            conv_terms.append(
                jnp.einsum(
                    "dfpc,dfpx->dcx",
                    padded[:, offset : offset + frames],
                    grad_pre,
                    preferred_element_type=jnp.float32,
                )
            )
            grad_norm = grad_norm + jnp.einsum(
                "dfpx,dcx->dfpc",
                grad_pad[:, 2 - offset : 2 - offset + frames],
                conv_pair[:, offset],
                preferred_element_type=jnp.float32,
            )
        conv_acc = conv_acc + jnp.stack(conv_terms, 1)
        incoming_gradient = grad_out.astype(jnp.float32) + inv_rms * (
            grad_norm - normed * jnp.mean(grad_norm * normed, -1, keepdims=True)
        )
        incoming_gradient = incoming_gradient.astype(jnp.bfloat16)
        if current_clock_tick + 1 < ticks:
            downward_gradient_holder = from_behind(incoming_gradient[0], "pipe", -1)
            upward_gradient_holder = from_behind(incoming_gradient[1], "pipe", 1)
    down_total = jnp.concatenate([conv_acc[0], out_acc[0][None]], 0)
    up_total = jnp.concatenate([conv_acc[1], out_acc[1][None]], 0)
    down_sum, up_sum = lax.psum((down_total, up_total), ("tm", "dp"))
    value = up_sum
    for bit_pos in range(bit_count):
        value = from_partner(value.astype(jnp.bfloat16), "pipe", bit_pos).astype(value.dtype)
    total = down_sum + value
    row_count = (
        micro * video.shape[1] * lax.axis_size("dp") * frames * lax.axis_size("tm") * video.shape[3]
    )
    scale = 1.0 / math.sqrt(row_count)
    return ((total[:3] * scale)[None], (total[3] * scale)[None])


def solution(mesh):
    return jax.shard_map(
        body,
        mesh=mesh,
        in_specs=(
            P(None, "dp", "tm", None, None),
            P(None, "dp", "tm", None, None),
            P(None, "dp"),
            P("pipe", None, None, None),
            P("pipe", None, None),
        ),
        out_specs=(P("pipe", None, None, None), P("pipe", None, None)),
        check_vma=False,
    )
```

profile of v0, /device:TPU:24, one launch (start us, length us, event | category | flops | bytes accessed | tf_op | source)
XLA Modules:
  0.0 1158.5 jit_solution(2011999744393750065)
XLA Ops:
  8.5 10.8 collective-permute-start.1
  26.7 21.4 %collective-permute-done.2 = bf16[4,320,320]{2,1,0:T(8,128)(2,1)} collective-permute-done((bf16[4,320,320]{2,1,0:T(8,128)(2,1)S(1)}, bf16[4,320,320]{2,1,0:T(8,128)(2,1)}, u32[]{:S(2)}, u32[]{:S(2)}) %collective-permute-start.2) | collective-permute-done | bytes 819232 | tf_op jit(solution)/shard_map/ppermute | solution.py:26
  48.1 4.9 collective-permute-start.3
  53.4 20.6 %collective-permute-done.3 = bf16[4,320,320]{2,1,0:T(8,128)(2,1)S(1)} collective-permute-done((bf16[4,320,320]{2,1,0:T(8,128)(2,1)}, bf16[4,320,320]{2,1,0:T(8,128)(2,1)S(1)}, u32[]{:S(2)}, u32[]{:S(2)}) %collective-permute-start.3) | collective-permute-done | bytes 819232 | tf_op jit(solution)/shard_map/ppermute | solution.py:26
  83.4 4.3 collective-permute-done.5
  90.4 6.0 collective-permute-start.7
  105.0 4.3 collective-permute-done.9
  111.9 6.4 collective-permute-start.11
  126.6 4.3 collective-permute-done.13
  133.5 6.4 collective-permute-start.15
  151.9 6.4 collective-permute-start.19
  160.6 6.3 collective-permute-done.18
  171.8 6.2 collective-permute-start.20
  181.9 4.6 collective-permute-start.23
  192.7 6.4 collective-permute-start.24
  203.6 4.9 collective-permute-start.27
  214.0 6.4 collective-permute-start.28
  225.3 5.2 collective-permute-start.31
  236.7 6.2 collective-permute-start.32
  247.7 5.0 collective-permute-start.35
  259.1 641.5 %all-reduce.4 = bf16[4,320,320]{2,1,0:T(8,128)(2,1)} all-reduce(f32[4,320,320]{2,1,0:T(8,128)S(1)} %pad_maximum_fusion.1), channel_id=1, replica_groups=mesh['pipe'=4,'tm'=32,'dp'=4] {'tm','dp'}, use_global_device_ids=true, to_apply=%region_10.11 | all-reduce | flops 409600 | bytes 2457600 | tf_op jit(solution)/shard_map/psum | solution.py:198
  906.8 12.7 %collective-permute-done.36 = bf16[4,320,320]{2,1,0:T(8,128)(2,1)S(1)} collective-permute-done((bf16[4,320,320]{2,1,0:T(8,128)(2,1)}, bf16[4,320,320]{2,1,0:T(8,128)(2,1)S(1)}, u32[]{:S(2)}, u32[]{:S(2)}) %collective-permute-start.36) | collective-permute-done | bytes 819232 | tf_op jit(solution)/shard_map/ppermute | solution.py:26
  919.5 10.0 collective-permute-start.37
  929.5 218.4 %all-reduce.3.cloned.1.call-done = f32[4,320,320]{2,1,0:T(8,128)} async-done(((f32[4,320,320]{2,1,0:T(8,128)}), f32[4,320,320]{2,1,0:T(8,128)}) %all-reduce.3.cloned.1.call-update) | async-done | bytes 1638416 | tf_op jit(solution)/shard_map/psum | solution.py:198
  (225 shorter events, 113.1 us)
Async XLA Ops:
  7.2 1140.7 %all-reduce.3.cloned.1.call-start = ((), (), s32[]{:S(2)}) async-start(), calls=%async_computation | async-start | bytes 3932160 | tf_op jit(solution)/shard_map/psum | solution.py:198
  8.5 44.8 %collective-permute-start.1 = (bf16[2,1,64,320]{3,2,1,0:T(8,128)(2,1)S(1)}, bf16[2,1,64,320]{3,2,1,0:T(8,128)(2,1)S(1)}, u32[]{:S(2)}, u32[]{:S(2)}) collective-permute-start(bf16[2,1,64,320]{3,2,1,0:T(8,128)(2,1)S(1)} %get-tuple-element.91), channel_id=1, source_target_pairs={{4,0},{8,4},{12,8},{16,12},{20,16},{24,20},{28,24},{32,28},{36,32}... | collective-permute-start | bytes 245768 | tf_op jit(solution)/shard_map/ppermute | solution.py:18
  19.4 34.0 %collective-permute-start = (bf16[2,1,64,320]{3,2,1,0:T(8,128)(2,1)S(1)}, bf16[2,1,64,320]{3,2,1,0:T(8,128)(2,1)S(1)}, u32[]{:S(2)}, u32[]{:S(2)}) collective-permute-start(bf16[2,1,64,320]{3,2,1,0:T(8,128)(2,1)S(1)} %get-tuple-element.92), channel_id=1, source_target_pairs={{0,4},{4,8},{8,12},{12,16},{16,20},{20,24},{24,28},{28,32},{32,36}... | collective-permute-start | bytes 245768 | tf_op jit(solution)/shard_map/ppermute | solution.py:15
  22.8 25.3 %collective-permute-start.2 = (bf16[4,320,320]{2,1,0:T(8,128)(2,1)S(1)}, bf16[4,320,320]{2,1,0:T(8,128)(2,1)}, u32[]{:S(2)}, u32[]{:S(2)}) collective-permute-start(bf16[4,320,320]{2,1,0:T(8,128)(2,1)S(1)} %pad_maximum_fusion.2), channel_id=1, source_target_pairs={{0,128},{128,0},{256,384},{384,256},{1,129},{129,1},{257,385},{385... | collective-permute-start | bytes 2457608 | tf_op jit(solution)/shard_map/ppermute | solution.py:26
  48.1 25.9 %collective-permute-start.3 = (bf16[4,320,320]{2,1,0:T(8,128)(2,1)}, bf16[4,320,320]{2,1,0:T(8,128)(2,1)S(1)}, u32[]{:S(2)}, u32[]{:S(2)}) collective-permute-start(bf16[4,320,320]{2,1,0:T(8,128)(2,1)} %collective-permute-done.2), channel_id=1, source_target_pairs={{0,256},{128,384},{256,0},{384,128},{1,257},{129,385},{257,1},{385... | collective-permute-start | bytes 2457608 | tf_op jit(solution)/shard_map/ppermute | solution.py:26
  88.4 8.6 collective-permute-start.6
  90.4 8.2 collective-permute-start.7
  109.9 9.0 collective-permute-start.10
  111.9 8.6 collective-permute-start.11
  131.5 9.0 collective-permute-start.14
  133.5 8.6 collective-permute-start.15
  151.9 15.3 %collective-permute-start.19 = (bf16[2,1,64,320]{3,2,1,0:T(8,128)(2,1)S(1)}, bf16[2,1,64,320]{3,2,1,0:T(8,128)(2,1)S(1)}, u32[]{:S(2)}, u32[]{:S(2)}) collective-permute-start(bf16[2,1,64,320]{3,2,1,0:T(8,128)(2,1)S(1)} %get-tuple-element.75), channel_id=1, source_target_pairs={{4,0},{8,4},{12,8},{16,12},{20,16},{24,20},{28,24},{32,28},{36,32}... | collective-permute-start | bytes 245768 | tf_op jit(solution)/shard_map/ppermute | solution.py:18
  158.3 8.6 collective-permute-start.18
  169.6 8.6 collective-permute-start.21
  171.8 8.2 collective-permute-start.20
  189.8 9.4 collective-permute-start.25
  192.7 8.6 collective-permute-start.24
  211.8 9.2 collective-permute-start.29
  214.0 9.1 collective-permute-start.28
  225.3 8.1 collective-permute-start.31
  234.5 8.8 collective-permute-start.33
  236.7 8.4 collective-permute-start.32
  900.6 18.9 %collective-permute-start.36 = (bf16[4,320,320]{2,1,0:T(8,128)(2,1)}, bf16[4,320,320]{2,1,0:T(8,128)(2,1)S(1)}, u32[]{:S(2)}, u32[]{:S(2)}) collective-permute-start(bf16[4,320,320]{2,1,0:T(8,128)(2,1)} %all-reduce.4), channel_id=1, source_target_pairs={{0,128},{128,0},{256,384},{384,256},{1,129},{129,1},{257,385},{385... | collective-permute-start | bytes 2457608 | tf_op jit(solution)/shard_map/ppermute | solution.py:26
  919.5 228.5 %collective-permute-start.37 = (bf16[4,320,320]{2,1,0:T(8,128)(2,1)S(1)}, bf16[4,320,320]{2,1,0:T(8,128)(2,1)S(1)}, u32[]{:S(2)}, u32[]{:S(2)}) collective-permute-start(bf16[4,320,320]{2,1,0:T(8,128)(2,1)S(1)} %collective-permute-done.36), channel_id=1, source_target_pairs={{0,256},{128,384},{256,0},{384,128},{1,257},{129,385},{257,1},{385... | collective-permute-start | bytes 2457608 | tf_op jit(solution)/shard_map/ppermute | solution.py:26
  (21 other events, 225.7 us)
Sparse Core Ops, SparseCore 0:
  906.9 240.9 all-reduce.2
where the time goes:
time: 1160 us
  blocking collectives  641 us (55%)
  waiting for transfers between devices  323 us (28%)
  starting transfers between devices  143 us (12%)
  matrix products  18.2 us (2%)
  between operations  15.5 us (1%)
  other arithmetic  13.4 us (1%)
    psum x1, blocking collectives, body(): down_sum, up_sum = lax.psum((down_total, up_total), ('tm', 'dp'))  641 us
    psum x1, waiting for transfers between devices, body(): down_sum, up_sum = lax.psum((down_total, up_total), ('tm', 'dp'))  218 us
    ppermute x9, starting transfers between devices, padded_2(): lax.ppermute(lax.slice_in_dim(block, 0, width, axis=dim), axis, backward)  61.4 us
    ppermute x4, waiting for transfers between devices, from_partner(): return lax.ppermute(value, axis, pairs)  54.6 us
    ppermute x16, starting transfers between devices, from_behind(): return lax.ppermute(array, axis, pairs)  41.9 us
    ppermute x16, waiting for transfers between devices, from_behind(): return lax.ppermute(array, axis, pairs)  29.7 us
  transfers between devices with their start and end apart: 39, of which 33 were waited for; matrix products, arithmetic and copies ran while one was open for 1% of the time, Pallas kernels for 0%

commit v1 on v0

--- a/solution.py
+++ b/solution.py
@@ -3,6 +3,7 @@
 import jax.numpy as jnp
 from jax import lax
 from jax.sharding import PartitionSpec as P
+from jax.lax import psum
 
 EPSILON = 1e-06
 
@@ -195,7 +196,13 @@
             upward_gradient_holder = from_behind(incoming_gradient[1], "pipe", 1)
     down_total = jnp.concatenate([conv_acc[0], out_acc[0][None]], 0)
     up_total = jnp.concatenate([conv_acc[1], out_acc[1][None]], 0)
-    down_sum, up_sum = lax.psum((down_total, up_total), ("tm", "dp"))
+
+    def drive_matrix(work_x, mesh_ax, comm_axis):
+        for k in (mesh_ax, comm_axis):
+            work_x = psum(work_x, k)
+        return work_x
+
+    down_sum, up_sum = drive_matrix((down_total, up_total), "tm", "dp")
     value = up_sum
     for bit_pos in range(bit_count):
         value = from_partner(value.astype(jnp.bfloat16), "pipe", bit_pos).astype(value.dtype)

time: 1160 us -> 743 us (0.64)
  the two profiles are of different devices: /device:TPU:24 before, /device:TPU:56 now
where the time goes in v1:
time: 743 us; the launch traced here: 742 us
  waiting for transfers between devices  449 us (60%)
  starting transfers between devices  138 us (19%)
  blocking collectives  104 us (14%)
  matrix products  18.3 us (2%)
  between operations  15.5 us (2%)
  other arithmetic  13.1 us (2%)
    psum x2, waiting for transfers between devices, drive_matrix(): work_x = psum(work_x, k)  324 us
    psum x1, blocking collectives, drive_matrix(): work_x = psum(work_x, k)  104 us
    ppermute x4, waiting for transfers between devices, from_partner(): return lax.ppermute(value, axis, pairs)  75.7 us
    ppermute x9, starting transfers between devices, padded_2(): lax.ppermute(lax.slice_in_dim(block, 0, width, axis=dim), axis, backward)  62.3 us
    ppermute x16, starting transfers between devices, from_behind(): return lax.ppermute(array, axis, pairs)  41.9 us
    ppermute x16, waiting for transfers between devices, from_behind(): return lax.ppermute(array, axis, pairs)  29.8 us
    ppermute x9, starting transfers between devices, padded_2(): lax.ppermute(lax.slice_in_dim(block, block.shape[dim] - width, None, axis...  17.3 us
    ppermute x4, starting transfers between devices, from_partner(): return lax.ppermute(value, axis, pairs)  16.7 us
  transfers between devices with their start and end apart: 40, of which 35 were waited for; matrix products, arithmetic and copies ran while one was open for 1% of the time, Pallas kernels for 0%

profile of v1, /device:TPU:56, one launch (start us, length us, event | category | flops | bytes accessed | tf_op | source)
XLA Modules:
  0.0 742.1 jit_solution(5268657340023033214)
XLA Ops:
  8.5 11.7 %collective-permute-start.1 = (bf16[2,1,64,320]{3,2,1,0:T(8,128)(2,1)S(1)}, bf16[2,1,64,320]{3,2,1,0:T(8,128)(2,1)S(1)}, u32[]{:S(2)}, u32[]{:S(2)}) collective-permute-start(bf16[2,1,64,320]{3,2,1,0:T(8,128)(2,1)S(1)} %get-tuple-element.93), channel_id=1, source_target_pairs={{4,0},{8,4},{12,8},{16,12},{20,16},{24,20},{28,24},{32,28},{36,32}... | collective-permute-start | bytes 245768 | tf_op jit(solution)/shard_map/ppermute | solution.py:19
  27.6 21.4 %collective-permute-done.2 = bf16[4,320,320]{2,1,0:T(8,128)(2,1)} collective-permute-done((bf16[4,320,320]{2,1,0:T(8,128)(2,1)S(1)}, bf16[4,320,320]{2,1,0:T(8,128)(2,1)}, u32[]{:S(2)}, u32[]{:S(2)}) %collective-permute-start.2) | collective-permute-done | bytes 819232 | tf_op jit(solution)/shard_map/ppermute | solution.py:27
  49.0 4.9 collective-permute-start.3
  54.3 20.6 %collective-permute-done.3 = bf16[4,320,320]{2,1,0:T(8,128)(2,1)S(1)} collective-permute-done((bf16[4,320,320]{2,1,0:T(8,128)(2,1)}, bf16[4,320,320]{2,1,0:T(8,128)(2,1)S(1)}, u32[]{:S(2)}, u32[]{:S(2)}) %collective-permute-start.3) | collective-permute-done | bytes 819232 | tf_op jit(solution)/shard_map/ppermute | solution.py:27
  89.5 6.0 collective-permute-start.7
  104.1 4.3 collective-permute-done.9
  111.0 6.4 collective-permute-start.11
  132.6 6.4 collective-permute-start.15
  151.0 6.4 collective-permute-start.19
  159.7 6.3 collective-permute-done.18
  170.9 6.2 collective-permute-start.20
  181.0 4.6 collective-permute-start.23
  191.8 6.4 collective-permute-start.24
  202.7 4.9 collective-permute-start.27
  213.1 6.4 collective-permute-start.28
  224.4 5.2 collective-permute-start.31
  235.9 6.2 collective-permute-start.32
  246.9 5.0 collective-permute-start.35
  259.8 314.2 %all-reduce.7.cloned.1.call-done = (f32[4,320,320]{2,1,0:T(8,128)}, f32[4,320,320]{2,1,0:T(8,128)}) async-done(((f32[4,320,320]{2,1,0:T(8,128)}, f32[4,320,320]{2,1,0:T(8,128)}), (f32[4,320,320]{2,1,0:T(8,128)}, f32[4,320,320]{2,1,0:T(8,128)})) %all-reduce.7.cloned.1.call-update) | async-done | bytes 3276816 | tf_op jit(solution)/shard_map/psum | solution.py:202
  575.5 104.1 %all-reduce.8 = bf16[4,320,320]{2,1,0:T(8,128)(2,1)S(1)} all-reduce(f32[4,320,320]{2,1,0:T(8,128)S(1)} %copy-done.1), channel_id=1, replica_groups=mesh['pipe'=4,'tm'=32,'dp'=4] {'dp'}, use_global_device_ids=true, to_apply=%region_12.13 | all-reduce | flops 409600 | bytes 2457600 | tf_op jit(solution)/shard_map/psum | solution.py:202
  683.0 22.2 %collective-permute-done.36 = bf16[4,320,320]{2,1,0:T(8,128)(2,1)S(1)} collective-permute-done((bf16[4,320,320]{2,1,0:T(8,128)(2,1)S(1)}, bf16[4,320,320]{2,1,0:T(8,128)(2,1)S(1)}, u32[]{:S(2)}, u32[]{:S(2)}) %collective-permute-start.36) | collective-permute-done | bytes 819232 | tf_op jit(solution)/shard_map/ppermute | solution.py:27
  705.2 4.9 collective-permute-start.37
  710.1 9.9 %all-reduce.5.cloned.1.call-done = f32[4,320,320]{2,1,0:T(8,128)} async-done(((f32[4,320,320]{2,1,0:T(8,128)}), f32[4,320,320]{2,1,0:T(8,128)}) %all-reduce.5.cloned.1.call-update) | async-done | bytes 1638416 | tf_op jit(solution)/shard_map/psum | solution.py:202
  720.0 11.5 %collective-permute-done.37 = bf16[4,320,320]{2,1,0:T(8,128)(2,1)S(1)} collective-permute-done((bf16[4,320,320]{2,1,0:T(8,128)(2,1)S(1)}, bf16[4,320,320]{2,1,0:T(8,128)(2,1)S(1)}, u32[]{:S(2)}, u32[]{:S(2)}) %collective-permute-start.37) | collective-permute-done | bytes 819232 | tf_op jit(solution)/shard_map/ppermute | solution.py:27
  (227 shorter events, 120.2 us)
Async XLA Ops:
  7.2 566.8 %all-reduce.7.cloned.1.call-start = ((), (), s32[]{:S(2)}) async-start(), calls=%async_computation.1 | async-start | bytes 7864320 | tf_op jit(solution)/shard_map/psum | solution.py:202
  8.5 45.7 %collective-permute-start.1 = (bf16[2,1,64,320]{3,2,1,0:T(8,128)(2,1)S(1)}, bf16[2,1,64,320]{3,2,1,0:T(8,128)(2,1)S(1)}, u32[]{:S(2)}, u32[]{:S(2)}) collective-permute-start(bf16[2,1,64,320]{3,2,1,0:T(8,128)(2,1)S(1)} %get-tuple-element.93), channel_id=1, source_target_pairs={{4,0},{8,4},{12,8},{16,12},{20,16},{24,20},{28,24},{32,28},{36,32}... | collective-permute-start | bytes 245768 | tf_op jit(solution)/shard_map/ppermute | solution.py:19
  20.3 34.0 %collective-permute-start = (bf16[2,1,64,320]{3,2,1,0:T(8,128)(2,1)S(1)}, bf16[2,1,64,320]{3,2,1,0:T(8,128)(2,1)S(1)}, u32[]{:S(2)}, u32[]{:S(2)}) collective-permute-start(bf16[2,1,64,320]{3,2,1,0:T(8,128)(2,1)S(1)} %get-tuple-element.94), channel_id=1, source_target_pairs={{0,4},{4,8},{8,12},{12,16},{16,20},{20,24},{24,28},{28,32},{32,36}... | collective-permute-start | bytes 245768 | tf_op jit(solution)/shard_map/ppermute | solution.py:16
  23.6 25.3 %collective-permute-start.2 = (bf16[4,320,320]{2,1,0:T(8,128)(2,1)S(1)}, bf16[4,320,320]{2,1,0:T(8,128)(2,1)}, u32[]{:S(2)}, u32[]{:S(2)}) collective-permute-start(bf16[4,320,320]{2,1,0:T(8,128)(2,1)S(1)} %pad_maximum_fusion.2), channel_id=1, source_target_pairs={{0,128},{128,0},{256,384},{384,256},{1,129},{129,1},{257,385},{385... | collective-permute-start | bytes 2457608 | tf_op jit(solution)/shard_map/ppermute | solution.py:27
  49.0 25.9 %collective-permute-start.3 = (bf16[4,320,320]{2,1,0:T(8,128)(2,1)}, bf16[4,320,320]{2,1,0:T(8,128)(2,1)S(1)}, u32[]{:S(2)}, u32[]{:S(2)}) collective-permute-start(bf16[4,320,320]{2,1,0:T(8,128)(2,1)} %collective-permute-done.2), channel_id=1, source_target_pairs={{0,256},{128,384},{256,0},{384,128},{1,257},{129,385},{257,1},{385... | collective-permute-start | bytes 2457608 | tf_op jit(solution)/shard_map/ppermute | solution.py:27
  87.5 8.6 %collective-permute-start.6 = (bf16[2,1,64,320]{3,2,1,0:T(8,128)(2,1)S(1)}, bf16[2,1,64,320]{3,2,1,0:T(8,128)(2,1)S(1)}, u32[]{:S(2)}, u32[]{:S(2)}) collective-permute-start(bf16[2,1,64,320]{3,2,1,0:T(8,128)(2,1)S(1)} %get-tuple-element.90), channel_id=1, source_target_pairs={{0,4},{4,8},{8,12},{12,16},{16,20},{20,24},{24,28},{28,32},{32,36}... | collective-permute-start | bytes 245768 | tf_op jit(solution)/shard_map/ppermute | solution.py:16
  89.5 8.2 %collective-permute-start.7 = (bf16[2,1,64,320]{3,2,1,0:T(8,128)(2,1)S(1)}, bf16[2,1,64,320]{3,2,1,0:T(8,128)(2,1)S(1)}, u32[]{:S(2)}, u32[]{:S(2)}) collective-permute-start(bf16[2,1,64,320]{3,2,1,0:T(8,128)(2,1)S(1)} %get-tuple-element.89), channel_id=1, source_target_pairs={{4,0},{8,4},{12,8},{16,12},{20,16},{24,20},{28,24},{32,28},{36,32}... | collective-permute-start | bytes 245768 | tf_op jit(solution)/shard_map/ppermute | solution.py:19
  109.0 9.0 %collective-permute-start.10 = (bf16[2,1,64,320]{3,2,1,0:T(8,128)(2,1)S(1)}, bf16[2,1,64,320]{3,2,1,0:T(8,128)(2,1)S(1)}, u32[]{:S(2)}, u32[]{:S(2)}) collective-permute-start(bf16[2,1,64,320]{3,2,1,0:T(8,128)(2,1)S(1)} %get-tuple-element.86), channel_id=1, source_target_pairs={{0,4},{4,8},{8,12},{12,16},{16,20},{20,24},{24,28},{28,32},{32,36}... | collective-permute-start | bytes 245768 | tf_op jit(solution)/shard_map/ppermute | solution.py:16
  111.0 8.6 %collective-permute-start.11 = (bf16[2,1,64,320]{3,2,1,0:T(8,128)(2,1)S(1)}, bf16[2,1,64,320]{3,2,1,0:T(8,128)(2,1)S(1)}, u32[]{:S(2)}, u32[]{:S(2)}) collective-permute-start(bf16[2,1,64,320]{3,2,1,0:T(8,128)(2,1)S(1)} %get-tuple-element.85), channel_id=1, source_target_pairs={{4,0},{8,4},{12,8},{16,12},{20,16},{24,20},{28,24},{32,28},{36,32}... | collective-permute-start | bytes 245768 | tf_op jit(solution)/shard_map/ppermute | solution.py:19
  130.6 9.0 %collective-permute-start.14 = (bf16[2,1,64,320]{3,2,1,0:T(8,128)(2,1)S(1)}, bf16[2,1,64,320]{3,2,1,0:T(8,128)(2,1)S(1)}, u32[]{:S(2)}, u32[]{:S(2)}) collective-permute-start(bf16[2,1,64,320]{3,2,1,0:T(8,128)(2,1)S(1)} %get-tuple-element.82), channel_id=1, source_target_pairs={{0,4},{4,8},{8,12},{12,16},{16,20},{20,24},{24,28},{28,32},{32,36}... | collective-permute-start | bytes 245768 | tf_op jit(solution)/shard_map/ppermute | solution.py:16
  132.6 8.6 %collective-permute-start.15 = (bf16[2,1,64,320]{3,2,1,0:T(8,128)(2,1)S(1)}, bf16[2,1,64,320]{3,2,1,0:T(8,128)(2,1)S(1)}, u32[]{:S(2)}, u32[]{:S(2)}) collective-permute-start(bf16[2,1,64,320]{3,2,1,0:T(8,128)(2,1)S(1)} %get-tuple-element.81), channel_id=1, source_target_pairs={{4,0},{8,4},{12,8},{16,12},{20,16},{24,20},{28,24},{32,28},{36,32}... | collective-permute-start | bytes 245768 | tf_op jit(solution)/shard_map/ppermute | solution.py:19
  151.0 15.3 %collective-permute-start.19 = (bf16[2,1,64,320]{3,2,1,0:T(8,128)(2,1)S(1)}, bf16[2,1,64,320]{3,2,1,0:T(8,128)(2,1)S(1)}, u32[]{:S(2)}, u32[]{:S(2)}) collective-permute-start(bf16[2,1,64,320]{3,2,1,0:T(8,128)(2,1)S(1)} %get-tuple-element.77), channel_id=1, source_target_pairs={{4,0},{8,4},{12,8},{16,12},{20,16},{24,20},{28,24},{32,28},{36,32}... | collective-permute-start | bytes 245768 | tf_op jit(solution)/shard_map/ppermute | solution.py:19
  157.4 8.6 %collective-permute-start.18 = (bf16[2,1,64,320]{3,2,1,0:T(8,128)(2,1)S(1)}, bf16[2,1,64,320]{3,2,1,0:T(8,128)(2,1)S(1)}, u32[]{:S(2)}, u32[]{:S(2)}) collective-permute-start(bf16[2,1,64,320]{3,2,1,0:T(8,128)(2,1)S(1)} %get-tuple-element.78), channel_id=1, source_target_pairs={{0,4},{4,8},{8,12},{12,16},{16,20},{20,24},{24,28},{28,32},{32,36}... | collective-permute-start | bytes 245768 | tf_op jit(solution)/shard_map/ppermute | solution.py:16
  168.6 8.6 %collective-permute-start.21 = (bf16[2,1,64,320]{3,2,1,0:T(8,128)(2,1)S(1)}, bf16[2,1,64,320]{3,2,1,0:T(8,128)(2,1)S(1)}, u32[]{:S(2)}, u32[]{:S(2)}) collective-permute-start(bf16[2,1,64,320]{3,2,1,0:T(8,128)(2,1)S(1)} %get-tuple-element.76), channel_id=1, source_target_pairs={{0,4},{4,8},{8,12},{12,16},{16,20},{20,24},{24,28},{28,32},{32,36}... | collective-permute-start | bytes 245768 | tf_op jit(solution)/shard_map/ppermute | solution.py:16
  170.9 8.2 %collective-permute-start.20 = (bf16[2,1,64,320]{3,2,1,0:T(8,128)(2,1)S(1)}, bf16[2,1,64,320]{3,2,1,0:T(8,128)(2,1)S(1)}, u32[]{:S(2)}, u32[]{:S(2)}) collective-permute-start(bf16[2,1,64,320]{3,2,1,0:T(8,128)(2,1)S(1)} %get-tuple-element.75), channel_id=1, source_target_pairs={{4,0},{8,4},{12,8},{16,12},{20,16},{24,20},{28,24},{32,28},{36,32}... | collective-permute-start | bytes 245768 | tf_op jit(solution)/shard_map/ppermute | solution.py:19
  188.8 9.4 %collective-permute-start.25 = (bf16[2,1,64,320]{3,2,1,0:T(8,128)(2,1)S(1)}, bf16[2,1,64,320]{3,2,1,0:T(8,128)(2,1)S(1)}, u32[]{:S(2)}, u32[]{:S(2)}) collective-permute-start(bf16[2,1,64,320]{3,2,1,0:T(8,128)(2,1)S(1)} %get-tuple-element.72), channel_id=1, source_target_pairs={{0,4},{4,8},{8,12},{12,16},{16,20},{20,24},{24,28},{28,32},{32,36}... | collective-permute-start | bytes 245768 | tf_op jit(solution)/shard_map/ppermute | solution.py:16
  191.8 8.6 %collective-permute-start.24 = (bf16[2,1,64,320]{3,2,1,0:T(8,128)(2,1)S(1)}, bf16[2,1,64,320]{3,2,1,0:T(8,128)(2,1)S(1)}, u32[]{:S(2)}, u32[]{:S(2)}) collective-permute-start(bf16[2,1,64,320]{3,2,1,0:T(8,128)(2,1)S(1)} %get-tuple-element.71), channel_id=1, source_target_pairs={{4,0},{8,4},{12,8},{16,12},{20,16},{24,20},{28,24},{32,28},{36,32}... | collective-permute-start | bytes 245768 | tf_op jit(solution)/shard_map/ppermute | solution.py:19
  210.9 9.2 %collective-permute-start.29 = (bf16[2,1,64,320]{3,2,1,0:T(8,128)(2,1)S(1)}, bf16[2,1,64,320]{3,2,1,0:T(8,128)(2,1)S(1)}, u32[]{:S(2)}, u32[]{:S(2)}) collective-permute-start(bf16[2,1,64,320]{3,2,1,0:T(8,128)(2,1)S(1)} %get-tuple-element.68), channel_id=1, source_target_pairs={{0,4},{4,8},{8,12},{12,16},{16,20},{20,24},{24,28},{28,32},{32,36}... | collective-permute-start | bytes 245768 | tf_op jit(solution)/shard_map/ppermute | solution.py:16
  213.1 9.0 %collective-permute-start.28 = (bf16[2,1,64,320]{3,2,1,0:T(8,128)(2,1)S(1)}, bf16[2,1,64,320]{3,2,1,0:T(8,128)(2,1)S(1)}, u32[]{:S(2)}, u32[]{:S(2)}) collective-permute-start(bf16[2,1,64,320]{3,2,1,0:T(8,128)(2,1)S(1)} %get-tuple-element.67), channel_id=1, source_target_pairs={{4,0},{8,4},{12,8},{16,12},{20,16},{24,20},{28,24},{32,28},{36,32}... | collective-permute-start | bytes 245768 | tf_op jit(solution)/shard_map/ppermute | solution.py:19
  233.6 8.8 %collective-permute-start.33 = (bf16[2,1,64,320]{3,2,1,0:T(8,128)(2,1)S(1)}, bf16[2,1,64,320]{3,2,1,0:T(8,128)(2,1)S(1)}, u32[]{:S(2)}, u32[]{:S(2)}) collective-permute-start(bf16[2,1,64,320]{3,2,1,0:T(8,128)(2,1)S(1)} %get-tuple-element.64), channel_id=1, source_target_pairs={{0,4},{4,8},{8,12},{12,16},{16,20},{20,24},{24,28},{28,32},{32,36}... | collective-permute-start | bytes 245768 | tf_op jit(solution)/shard_map/ppermute | solution.py:16
  235.9 8.4 %collective-permute-start.32 = (bf16[2,1,64,320]{3,2,1,0:T(8,128)(2,1)S(1)}, bf16[2,1,64,320]{3,2,1,0:T(8,128)(2,1)S(1)}, u32[]{:S(2)}, u32[]{:S(2)}) collective-permute-start(bf16[2,1,64,320]{3,2,1,0:T(8,128)(2,1)S(1)} %get-tuple-element.63), channel_id=1, source_target_pairs={{4,0},{8,4},{12,8},{16,12},{20,16},{24,20},{28,24},{32,28},{36,32}... | collective-permute-start | bytes 245768 | tf_op jit(solution)/shard_map/ppermute | solution.py:19
  259.7 460.3 %all-reduce.5.cloned.1.call-start = ((), (), s32[]{:S(2)}) async-start(), calls=%async_computation | async-start | bytes 3932160 | tf_op jit(solution)/shard_map/psum | solution.py:202
  679.6 25.6 %collective-permute-start.36 = (bf16[4,320,320]{2,1,0:T(8,128)(2,1)S(1)}, bf16[4,320,320]{2,1,0:T(8,128)(2,1)S(1)}, u32[]{:S(2)}, u32[]{:S(2)}) collective-permute-start(bf16[4,320,320]{2,1,0:T(8,128)(2,1)S(1)} %all-reduce.8), channel_id=1, source_target_pairs={{0,128},{128,0},{256,384},{384,256},{1,129},{129,1},{257,385},{385... | collective-permute-start | bytes 2457608 | tf_op jit(solution)/shard_map/ppermute | solution.py:27
  705.2 26.4 %collective-permute-start.37 = (bf16[4,320,320]{2,1,0:T(8,128)(2,1)S(1)}, bf16[4,320,320]{2,1,0:T(8,128)(2,1)S(1)}, u32[]{:S(2)}, u32[]{:S(2)}) collective-permute-start(bf16[4,320,320]{2,1,0:T(8,128)(2,1)S(1)} %collective-permute-done.36), channel_id=1, source_target_pairs={{0,256},{128,384},{256,0},{384,128},{1,257},{129,385},{257,1},{385... | collective-permute-start | bytes 2457608 | tf_op jit(solution)/shard_map/ppermute | solution.py:27
  (22 other events, 235.5 us)
Sparse Core Ops, SparseCore 0:
  259.8 314.0 all-reduce.6
  577.2 142.7 all-reduce.4
